TPU v7x, 512 devices: a whole 4x8x8 slice. The times are simulated.
512 devices in a mesh: grp: 64 (over y, z_hi, core), tp: 8 (over x, z_lo).
Axes of the slice: x: 4, y: 8, z: 8 (z_hi: 4, z_lo: 2; z = z_hi * 2 + z_lo), core: 2. Of those that a mesh axis runs over, the one named last changes fastest.
Arguments:
- learn_rows: bfloat16 [98304, 5120], P('grp', 'tp'), may hold values from -6 to 6
- cot_values: bfloat16 [98304, 1024], P('grp', 'tp'), may hold values from -60 to 60
- rewards: float32 [98304], P('grp'), may hold values from 0 to 4
- group_ids: int32 [98304], P('grp'), may hold values from 0 to 255
- master: float32 [1024, 5120], P('grp', 'tp'), may hold values from -0.078125 to 0.078125
- moment_one: float32 [1024, 5120], P('grp', 'tp'), may hold values from -2 to 2
- moment_two: float32 [1024, 5120], P('grp', 'tp'), may hold values from 0.041666668 to 4.1666665
- decode_rows: bfloat16 [512, 5120], P('grp'), may hold values from -6 to 6
- queries: bfloat16 [512, 8192], P('grp', 'tp'), may hold values from -100 to 100
- fresh_keys: bfloat16 [512, 1024], P('grp', 'tp'), may hold values from -4.04 to 4.04
- stored_keys: bfloat16 [512, 256, 1024], P('grp', None, 'tp'), may hold values from -4 to 4
- stored_values: bfloat16 [512, 256, 1024], P('grp', None, 'tp'), may hold values from -6 to 6
- cache_lengths: int32 [512], P('grp'), may hold values from 1 to 256, as said below
Outputs:
- new_master: float32 [1024, 5120], P('grp', 'tp')
- new_moment_one: float32 [1024, 5120], P('grp', 'tp')
- new_moment_two: float32 [1024, 5120], P('grp', 'tp')
- attended: bfloat16 [512, 8192], P('grp', 'tp')
Inputs may be any that keep to these rules, and one draw needn't show every extreme that they name: `cache_lengths`: row 0 of every draw holds 256.
All inputs are finite; a program needn't handle non-finite values.
Results may differ from a plain program's by a relative error of at most 0.013.
Values may be sent and summed in bfloat16 or wider, within the bound.
A program may use at most 64 MiB of HBM per device.

v0:
```python
import math

import jax
import jax.numpy as jnp
from jax import lax
from jax.sharding import PartitionSpec as P

QUERY_HEADS = 64
KEY_VALUE_HEADS = 8
HEAD_SIZE = 128
LROWS_DEV = 1536
GROUPS_DEV = 4


beta_one = 0.9
beta_two = 0.95
learning_rate = 0.001
weight_decay = 0.1
adam_epsilon = 1e-08
step_count = 2.0


def per_device(
    learn_rows,
    cot_values,
    rewards,
    group_ids,
    master,
    moment_one,
    moment_two,
    decode_rows,
    queries,
    fresh_keys,
    stored_keys,
    stored_values,
    cache_lengths,
):
    highest = lax.Precision.HIGHEST
    group_count = GROUPS_DEV * lax.axis_size("grp")
    onehot = (group_ids[:, None] == jnp.arange(group_count, dtype=jnp.int32)[None, :]).astype(
        jnp.float32
    )
    local_totals = jnp.dot(rewards, onehot, precision=highest)
    local_members = jnp.sum(onehot, axis=0)
    totals, members = lax.psum((local_totals, local_members), "grp")
    advantage = rewards - jnp.dot(onehot, totals, precision=highest) / jnp.dot(
        onehot, members, precision=highest
    )
    weighted = (advantage[:, None] * cot_values.astype(jnp.float32) / LROWS_DEV).astype(
        jnp.bfloat16
    )
    every_column = lax.all_gather(weighted, "tp", axis=1, tiled=True)
    gradient = lax.psum_scatter(
        lax.dot_general(
            every_column, learn_rows, (((0,), (0,)), ((), ())), preferred_element_type=jnp.float32
        ),
        "grp",
        scatter_dimension=0,
        tiled=True,
    )
    first = beta_one * moment_one + (1.0 - beta_one) * gradient
    second = beta_two * moment_two + (1.0 - beta_two) * gradient * gradient
    first_hat = first / (1.0 - beta_one**step_count)
    second_hat = second / (1.0 - beta_two**step_count)
    updated = master - learning_rate * (
        first_hat / (jnp.sqrt(second_hat) + adam_epsilon) + weight_decay * master
    )
    refreshed = updated.astype(jnp.bfloat16)
    kv_local = fresh_keys.shape[1] // HEAD_SIZE
    full_width = lax.all_gather(refreshed, "tp", axis=1, tiled=True)
    whole_matrix = lax.all_gather(full_width, "grp", axis=0, tiled=True)
    head_width = whole_matrix.shape[0] // lax.axis_size("tp")
    head_rows = lax.dynamic_slice_in_dim(
        whole_matrix, lax.axis_index("tp") * head_width, head_width, 0
    )
    fresh_values = lax.dot_general(
        decode_rows, head_rows, (((1,), (1,)), ((), ())), preferred_element_type=jnp.float32
    ).astype(jnp.bfloat16)
    row_sum_total = queries.shape[0]
    heads_per_group = QUERY_HEADS // KEY_VALUE_HEADS
    positions = stored_keys.shape[1]
    scale_factor = 1.0 / math.sqrt(HEAD_SIZE)
    query_tiles = queries.reshape(row_sum_total, kv_local, heads_per_group, HEAD_SIZE)
    key_tiles = stored_keys.reshape(row_sum_total, positions, kv_local, HEAD_SIZE)
    value_tiles = stored_values.reshape(row_sum_total, positions, kv_local, HEAD_SIZE)
    scores = (
        jnp.einsum("rhgd,rlhd->rhgl", query_tiles, key_tiles, preferred_element_type=jnp.float32)
        * scale_factor
    )
    visible = (jnp.arange(positions, dtype=jnp.int32)[None, :] < cache_lengths[:, None])[
        :, None, None, :
    ]
    scores = jnp.where(visible, scores, -jnp.inf)
    self_score = (
        jnp.einsum(
            "qvpb,qvb->qvp",
            query_tiles,
            fresh_keys.reshape(row_sum_total, kv_local, HEAD_SIZE),
            preferred_element_type=jnp.float32,
        )
        * scale_factor
    )
    highest_score = jnp.maximum(jnp.max(scores, axis=-1), self_score)
    cache_exp = jnp.exp(scores - highest_score[..., None])
    own_exp = jnp.exp(self_score - highest_score)
    denominator = jnp.sum(cache_exp, axis=-1) + own_exp
    cache_weights = (cache_exp / denominator[..., None]).astype(jnp.bfloat16)
    self_weight = (own_exp / denominator).astype(jnp.bfloat16)
    output_rows = jnp.einsum(
        "rhgl,rlhd->rhgd", cache_weights, value_tiles, preferred_element_type=jnp.float32
    )
    output_rows = output_rows + self_weight.astype(jnp.float32)[..., None] * fresh_values.astype(
        jnp.float32
    ).reshape(row_sum_total, kv_local, 1, HEAD_SIZE)
    attended = output_rows.reshape(row_sum_total, kv_local * heads_per_group * HEAD_SIZE).astype(
        jnp.bfloat16
    )
    return (updated, first, second, attended)


def solution(mesh):
    in_specs = (
        P("grp", "tp"),
        P("grp", "tp"),
        P("grp"),
        P("grp"),
        P("grp", "tp"),
        P("grp", "tp"),
        P("grp", "tp"),
        P("grp", None),
        P("grp", "tp"),
        P("grp", "tp"),
        P("grp", None, "tp"),
        P("grp", None, "tp"),
        P("grp"),
    )
    out_specs = (P("grp", "tp"), P("grp", "tp"), P("grp", "tp"), P("grp", "tp"))
    return jax.shard_map(
        per_device, mesh=mesh, in_specs=in_specs, out_specs=out_specs, check_vma=False
    )
```

profile of v0, /device:TPU:7, one launch (start us, length us, event | category | flops | bytes accessed | tf_op | source)
XLA Modules:
  0.0 546.9 jit_solution(10961193447551792455)
XLA Ops:
  7.2 0.0 all-gather.3.cloned.1.call-start
  7.2 0.8 reshape.92
  8.1 1.0 convert_reduce_fusion
  9.0 1.3 fusion.2
  10.4 145.0 %all-reduce = (f32[256]{0:T(256)S(1)}, f32[256]{0:T(256)S(1)}) all-reduce(f32[256]{0:T(256)S(1)} %bitcast.27, f32[256]{0:T(256)S(1)} %convert_reduce_fusion), channel_id=1, replica_groups=mesh['grp'=64,'tp'=8] {'grp'}, use_global_device_ids=true, to_apply=%region_0.0 | all-reduce | flops 512 | bytes 4096 | tf_op jit(solution)/shard_map/psum | solution.py:45
  155.4 1.5 fusion.8
  156.9 1.5 fusion.9
  158.5 0.7 divide_subtract_fusion
  159.2 2.0 multiply_convert_fusion
  161.2 0.0 reduce-scatter.2.cloned.1.call-start
  161.3 74.6 %all-gather.3.cloned.1.call-done = bf16[1536,1024]{1,0:T(8,128)(2,1)} async-done(((bf16[1536,128]{1,0:T(8,128)(2,1)}), bf16[1536,1024]{1,0:T(8,128)(2,1)}) %all-gather.3.cloned.1.call-update) | async-done | bytes 3145744 | tf_op jit(solution)/shard_map/all_gather | solution.py:52
  235.9 6.1 %fusion.36 = f32[1024,640]{1,0:T(8,128)} fusion(bf16[1536,1024]{1,0:T(8,128)(2,1)} %all-gather.3.cloned.1.call-done, bf16[1536,640]{1,0:T(8,128)(2,1)S(1)} %copy-done), kind=kOutput, calls=%fused_computation.45 | convolution fusion | flops 2013265920 | bytes 7733248 | tf_op jit(solution)/shard_map/dot_general | solution.py:54
  242.1 0.0 all-gather.5.cloned.1.call-start
  242.1 149.3 %reduce-scatter.2.cloned.1.call-done = f32[16,640]{1,0:T(8,128)} async-done(((f32[1024,640]{1,0:T(8,128)}), f32[16,640]{1,0:T(8,128)}) %reduce-scatter.2.cloned.1.call-update) | async-done | bytes 40976 | tf_op jit(solution)/shard_map/reduce_scatter | solution.py:53
  391.4 1.4 fusion.33
  392.8 22.1 %all_gather.10 = bf16[16,5120]{1,0:T(8,128)(2,1)} all-gather(bf16[16,640]{1,0:T(8,128)(2,1)S(1)} %get-tuple-element.6), channel_id=1, replica_groups=mesh['grp'=64,'tp'=8] {'tp'}, dimensions={1}, use_global_device_ids=true | all-gather | bytes 184320 | tf_op jit(solution)/shard_map/all_gather | solution.py:70
  415.0 0.1 iota_compare_fusion.8
  415.1 0.1 fusion.26
  415.2 0.3 fusion.35
  415.5 0.2 fusion.22
  415.7 122.0 %all-gather.5.cloned.1.call-done = bf16[1024,5120]{1,0:T(8,128)(2,1)} async-done(((bf16[16,5120]{1,0:T(8,128)(2,1)}), bf16[1024,5120]{1,0:T(8,128)(2,1)}) %all-gather.5.cloned.1.call-update) | async-done | bytes 10485776 | tf_op jit(solution)/shard_map/all_gather | solution.py:71
  537.8 1.7 fusion.16
  539.5 0.3 fusion.7
  539.8 0.6 copy.31
  (25 shorter events, 0.1 us)
Async XLA Ops:
  7.2 228.7 %copy-start = (bf16[1536,640]{1,0:T(8,128)(2,1)S(1)}, bf16[1536,640]{1,0:T(8,128)(2,1)}, u32[]{:S(2)}) copy-start(bf16[1536,640]{1,0:T(8,128)(2,1)} %param.13) | copy-start | bytes 5898244
  7.2 228.7 %all-gather.3.cloned.1.call-start = ((), (), s32[]{:S(2)}) async-start(), calls=%async_computation.1 | async-start | bytes 3538944 | tf_op jit(solution)/shard_map/all_gather | solution.py:52
  161.2 230.2 %reduce-scatter.2.cloned.1.call-start = ((), (), s32[]{:S(2)}) async-start(), calls=%async_computation.2 | async-start | bytes 2662400 | tf_op jit(solution)/shard_map/reduce_scatter | solution.py:53
  242.0 149.4 %copy-start.3 = (f32[16,640]{1,0:T(8,128)S(1)}, f32[16,640]{1,0:T(8,128)}, u32[]{:S(2)}) copy-start(f32[16,640]{1,0:T(8,128)} %param.17) | copy-start | bytes 122884
  242.0 149.4 %copy-start.4 = (f32[16,640]{1,0:T(8,128)S(1)}, f32[16,640]{1,0:T(8,128)}, u32[]{:S(2)}) copy-start(f32[16,640]{1,0:T(8,128)} %param.18) | copy-start | bytes 122884
  242.0 149.4 %copy-start.5 = (f32[16,640]{1,0:T(8,128)S(1)}, f32[16,640]{1,0:T(8,128)}, u32[]{:S(2)}) copy-start(f32[16,640]{1,0:T(8,128)} %param.19) | copy-start | bytes 122884
  242.0 173.0 %copy-start.7 = (s32[8]{0:T(128)S(1)}, s32[8]{0:T(128)}, u32[]{:S(2)}) copy-start(s32[8]{0:T(128)} %param.25) | copy-start | bytes 100
  242.0 173.1 %copy-start.6 = (bf16[8,1024]{1,0:T(8,128)(2,1)S(1)}, bf16[8,1024]{1,0:T(8,128)(2,1)}, u32[]{:S(2)}) copy-start(bf16[8,1024]{1,0:T(8,128)(2,1)} %param.21) | copy-start | bytes 49156
  242.0 173.1 %copy-start.9 = (bf16[8,128]{1,0:T(8,128)(2,1)S(1)}, bf16[8,128]{1,0:T(8,128)(2,1)}, u32[]{:S(2)}) copy-start(bf16[8,128]{1,0:T(8,128)(2,1)} %param.22) | copy-start | bytes 6148
  242.0 173.2 %copy-start.1 = (bf16[8,256,128]{2,1,0:T(8,128)(2,1)S(1)}, bf16[8,256,128]{2,1,0:T(8,128)(2,1)}, u32[]{:S(2)}) copy-start(bf16[8,256,128]{2,1,0:T(8,128)(2,1)} %param.23) | copy-start | bytes 1572868
  242.0 295.7 %copy-start.2 = (bf16[8,5120]{1,0:T(8,128)(2,1)S(1)}, bf16[8,5120]{1,0:T(8,128)(2,1)}, u32[]{:S(2)}) copy-start(bf16[8,5120]{1,0:T(8,128)(2,1)} %param.20) | copy-start | bytes 245764
  242.1 297.5 %copy-start.8 = (bf16[8,256,128]{2,1,0:T(8,128)(2,1)S(1)}, bf16[8,256,128]{2,1,0:T(8,128)(2,1)}, u32[]{:S(2)}) copy-start(bf16[8,256,128]{2,1,0:T(8,128)(2,1)} %param.24) | copy-start | bytes 1572868
  242.1 295.7 %all-gather.5.cloned.1.call-start = ((), (), s32[]{:S(2)}) async-start(), calls=%async_computation.3 | async-start | bytes 10649600 | tf_op jit(solution)/shard_map/all_gather | solution.py:71
Sparse Core Ops, SparseCore 0:
  161.3 74.5 all-gather.2
  242.2 149.1 reduce-scatter.1
  415.1 122.6 all-gather.4
where the time goes:
time: 548 us; the launch traced here: 547 us
  waiting for transfers between devices  346 us (63%)
  blocking collectives  167 us (30%)
  between operations  13.8 us (3%)
  matrix products  12.9 us (2%)
    reduce_scatter x1, waiting for transfers between devices, per_device(): lax.psum_scatter(lax.dot_general(every_column, learn_rows, (((0,), (0,)),...  149 us
    psum x1, blocking collectives, per_device(): totals, members = lax.psum((local_totals, local_members), 'grp')  145 us
    all_gather x1, waiting for transfers between devices, per_device(): whole_matrix = lax.all_gather(full_width, 'grp', axis=0, tiled=True)  122 us
    all_gather x1, waiting for transfers between devices, per_device(): every_column = lax.all_gather(weighted, 'tp', axis=1, tiled=True)  74.6 us
    all_gather x1, blocking collectives, per_device(): full_width = lax.all_gather(refreshed, 'tp', axis=1, tiled=True)  22.1 us
  transfers between devices with their start and end apart: 3, of which 3 were waited for; matrix products, arithmetic and copies ran while one was open for 0% of the time, Pallas kernels for 0%

commit v1 on v0

v1 whole, which is shorter than its diff:
```python
import math

import jax
import jax.numpy as jnp
from jax import lax
from jax.experimental import pallas as pl
from jax.experimental.pallas import tpu as pltpu
from jax.sharding import PartitionSpec as P

HEAD_SIZE = 128
QUERIES = 8
ROWS = 1536
WIDTH = 640
GROUPS = 256
SLOTS = 256
DECODE = 8
Y, ZH, CORE, X, ZL = 8, 4, 2, 4, 2
TP = X * ZL
BLOCKS = 8
BLOCK = 16
HALF = 64
WIDE = 3

beta_one = 0.9
beta_two = 0.95
learning_rate = 0.001
weight_decay = 0.1
adam_epsilon = 1e-08
step_count = 2.0

MESH = pl.DeviceIdType.MESH
bf16, f32 = jnp.bfloat16, jnp.float32


def split_three(value):
    high = value.astype(bf16)
    rest = value - high.astype(f32)
    middle = rest.astype(bf16)
    low = (rest - middle.astype(f32)).astype(bf16)
    return high, middle, low


def optimizer_step(gradient, master, moment_one, moment_two):
    first = beta_one * moment_one + (1.0 - beta_one) * gradient
    second = beta_two * moment_two + (1.0 - beta_two) * gradient * gradient
    first_hat = first / (1.0 - beta_one**step_count)
    second_hat = second / (1.0 - beta_two**step_count)
    updated = master - learning_rate * (
        first_hat / (jnp.sqrt(second_hat) + adam_epsilon) + weight_decay * master
    )
    return updated, first, second


def dot(a, b, dims):
    return lax.dot_general(a, b, (dims, ((), ())), preferred_element_type=f32)


def kernel(
    cot_hbm,
    learn_hbm,
    rewards_hbm,
    ids_hbm,
    master_hbm,
    one_hbm,
    two_hbm,
    decode_hbm,
    queries_hbm,
    fresh_hbm,
    keys_hbm,
    values_hbm,
    lengths_ref,
    gradient_hbm,
    attended_hbm,
    cot,
    learn,
    rewards,
    ids,
    adam_in,
    decode_own,
    queries,
    fresh,
    keys,
    values,
    attended,
    gathered,
    member,
    totals_out,
    totals_core,
    totals_z,
    totals_y,
    decode_all,
    weights,
    cache_part,
    own_part,
    kept,
    core_out,
    core_in,
    z_out,
    z_in,
    y_out,
    y_in,
    wide_out,
    wide_in,
    own_sum,
    fresh_rows,
    part_out,
    part_in,
    load_sem,
    store_sem,
    ag_send,
    ag_recv,
    core_send,
    core_recv,
    z_send,
    z_recv,
    y_send,
    y_recv,
    row_send,
    row_recv,
    part_send,
    part_recv,
    tot_send,
    tot_recv,
    dec_send,
    dec_recv,
):
    g, t = lax.axis_index("grp"), lax.axis_index("tp")
    y, zh, core = g // (ZH * CORE), lax.rem(g // CORE, ZH), lax.rem(g, CORE)
    x, zl = t // ZL, lax.rem(t, ZL)

    def grp_of(y_at, zh_at, core_at):
        return (y_at * ZH + zh_at) * CORE + core_at

    def tp_of(x_off, flip):
        return lax.rem(x + x_off + X, X) * ZL + lax.rem(zl + flip, ZL)

    right, left, across = tp_of(1, 0), tp_of(-1, 0), tp_of(0, 1)

    def remote(src, dst, send, recv, device):
        return pltpu.make_async_remote_copy(
            src_ref=src,
            dst_ref=dst,
            send_sem=send,
            recv_sem=recv,
            device_id=device,
            device_id_type=MESH,
        )

    loads = [
        (cot_hbm, cot),
        (ids_hbm, ids),
        (rewards_hbm, rewards),
        (queries_hbm, queries),
        (fresh_hbm, fresh),
        (keys_hbm, keys),
        (decode_hbm.at[:, pl.ds(pl.multiple_of(t * WIDTH, 128), WIDTH)], decode_own),
        (learn_hbm, learn),
        (values_hbm, values),
        (master_hbm, adam_in.at[0]),
        (one_hbm, adam_in.at[1]),
        (two_hbm, adam_in.at[2]),
    ]
    loads = [pltpu.make_async_copy(src, dst, load_sem.at[i]) for i, (src, dst) in enumerate(loads)]
    for load in loads:
        load.start()
    (l_cot, l_ids, l_rewards, l_queries, l_fresh, l_keys, l_decode, l_learn, l_values, *l_adam) = loads

    barrier = pltpu.get_barrier_semaphore()

    def greet(device):
        pl.semaphore_signal(barrier, inc=1, device_id=device, device_id_type=MESH)

    for peer in (right, left, across):
        greet((g, peer))
    greet((grp_of(y, zh, 1 - core), t))
    for d in range(1, ZH):
        greet((grp_of(y, lax.rem(zh + d, ZH), core), t))
    for d in range(1, Y):
        greet((grp_of(lax.rem(y + d, Y), zh, core), t))
    l_cot.wait()
    turned = cot[...].T
    gathered[pl.ds(t * BLOCKS, BLOCKS)] = turned.reshape(BLOCKS, BLOCK, ROWS)

    pl.semaphore_wait(barrier, 3 + 1 + (ZH - 1) + (Y - 1))

    xl, xr, xx = tp_of(-1, 0), tp_of(1, 0), tp_of(2, 0)
    zo, zxl, zxr, zxx = tp_of(0, 1), tp_of(-1, 1), tp_of(1, 1), tp_of(2, 1)
    pieces = {
        "z0": (across, t, zo, 2, 3),
        "z1": (across, t, zo, 5, 3),
        "z2": (across, t, zo, 0, 2),
        "z3": (across, xl, zxl, 0, 2),
        "z4": (across, xr, zxr, 0, 2),
        "z5": (across, xx, zxx, 0, 2),
        "r0": (right, t, xl, 0, 4),
        "r1": (right, t, xl, 4, 4),
        "r2": (right, xl, xx, 0, 4),
        "r3": (right, zo, zxl, 2, 3),
        "r4": (right, zo, zxl, 5, 3),
        "r5": (right, zxl, zxx, 2, 3),
        "l0": (left, t, xr, 4, 4),
        "l1": (left, t, xr, 0, 4),
        "l2": (left, xr, xx, 4, 4),
        "l3": (left, zo, zxr, 5, 3),
        "l4": (left, zo, zxr, 2, 3),
        "l5": (left, zxr, zxx, 5, 3),
    }
    order = list(pieces)

    def piece(name, landed):
        peer, source, lands, first, count = pieces[name]
        blocks = gathered.at[pl.ds((lands if landed else source) * BLOCKS + first, count)]
        n = order.index(name)
        return remote(blocks, blocks, ag_send.at[n], ag_recv.at[n], (g, peer))

    def send(*names):
        for name in names:
            piece(name, False).start()

    def arrived(*names):
        for name in names:
            piece(name, True).wait_recv()

    send("z0", "r0", "l0")

    l_ids.wait()
    l_rewards.wait()
    group_at = lax.broadcasted_iota(jnp.int32, (GROUPS, ROWS), 0)
    id_row = jnp.concatenate([ids[k : k + 1, :] for k in range(ROWS // 128)], axis=1)
    reward_row = jnp.concatenate([rewards[k : k + 1, :] for k in range(ROWS // 128)], axis=1)
    member[...] = jnp.where(group_at == id_row, 1.0, 0.0).astype(bf16)
    high, middle, low = split_three(reward_row)
    rows = lax.broadcasted_iota(jnp.int32, (8, ROWS), 0)
    stack = jnp.where(
        rows == 0,
        high.astype(f32),
        jnp.where(rows == 1, middle.astype(f32), jnp.where(rows == 2, low.astype(f32), 1.0)),
    )
    totals_out[0] = dot(stack.astype(bf16), member[...], ((1,), (1,)))
    totals_of_core = remote(
        totals_out.at[0], totals_core, tot_send.at[0], tot_recv.at[0], (grp_of(y, zh, 1 - core), t)
    )
    totals_of_core.start()
    send("r1", "l1")

    totals_of_core.wait_recv()
    totals_out[1] = totals_out[0] + totals_core[...]

    def totals_over_z(d, landed):
        to, source = lax.rem(zh + d, ZH), lax.rem(zh - d + ZH, ZH)
        return remote(
            totals_out.at[1],
            totals_z.at[source if landed else zh],
            tot_send.at[d],
            tot_recv.at[d],
            (grp_of(y, to, core), t),
        )

    for d in range(1, ZH):
        totals_over_z(d, False).start()
    send("z1", "z2")

    total = totals_out[1]
    for d in range(1, ZH):
        totals_over_z(d, True).wait_recv()
        total = total + totals_z[lax.rem(zh - d + ZH, ZH)]
    totals_out[2] = total

    def totals_over_y(d, landed):
        to, source = lax.rem(y + d, Y), lax.rem(y - d + Y, Y)
        return remote(
            totals_out.at[2],
            totals_y.at[source if landed else y],
            tot_send.at[ZH + d],
            tot_recv.at[ZH + d],
            (grp_of(to, zh, core), t),
        )

    for d in range(1, Y):
        totals_over_y(d, False).start()

    l_decode.wait()
    decode_all[core, y] = decode_own[...].astype(f32)

    def decode_copy(d, landed):
        to, source = lax.rem(y + d, Y), lax.rem(y - d + Y, Y)
        block = decode_all.at[core, source if landed else y]
        return remote(block, block, dec_send.at[d], dec_recv.at[d], (grp_of(to, zh, core), t))

    for d in range(1, Y):
        decode_copy(d, False).start()

    arrived("r0")
    send("r2", "z3")
    arrived("l0")
    send("l2")

    for d in range(1, Y):
        totals_over_y(d, True).wait_recv()
        total = total + totals_y[lax.rem(y - d + Y, Y)]

    size = total[3:4]
    mean = jnp.where(
        size > 0.5, (total[0:1] + total[1:2] + total[2:3]) / jnp.maximum(size, 1.0), 0.0
    )
    high, middle, low = split_three(mean)
    rows = lax.broadcasted_iota(jnp.int32, (8, GROUPS), 0)
    stack = jnp.where(
        rows == 0,
        high.astype(f32),
        jnp.where(rows == 1, middle.astype(f32), jnp.where(rows == 2, low.astype(f32), 0.0)),
    )
    means = dot(stack.astype(bf16), member[...], ((1,), (0,)))
    advantage = (reward_row - (means[0:1] + means[1:2] + means[2:3])) / float(ROWS)
    l_learn.wait()
    for k in range(ROWS // 128):
        column = jnp.broadcast_to(advantage[:, k * 128 : (k + 1) * 128], (128, 128)).T
        scaled = learn[k * 128 : (k + 1) * 128, :].astype(f32) * jnp.concatenate(
            [column] * (WIDTH // 128), axis=1
        )
        learn[k * 128 : (k + 1) * 128, :] = scaled.astype(bf16)

    def head_of(step):
        x_off = jnp.where(
            jnp.logical_or(step == 1, step == 5),
            X - 1,
            jnp.where(
                jnp.logical_or(step == 2, step == 6),
                1,
                jnp.where(jnp.logical_or(step == 4, step == 7), 2, 0),
            ),
        )
        flip = jnp.where(jnp.logical_or(step == 3, step >= 5), 1, 0)
        return tp_of(x_off, flip)

    def core_copy(step):
        return remote(
            core_out.at[step],
            core_in.at[step],
            core_send.at[step],
            core_recv.at[step],
            (grp_of(y, zh, 1 - core), t),
        )

    def z_copy(step, d, landed):
        to, source = lax.rem(zh + d, ZH), lax.rem(zh - d + ZH, ZH)
        return remote(
            z_out.at[step, to],
            z_in.at[step, source if landed else zh],
            z_send.at[step * ZH + d],
            z_recv.at[step * ZH + d],
            (grp_of(y, to, core), t),
        )

    def y_copy(step, head):
        return remote(
            y_out.at[step], y_in.at[y], y_send.at[step], y_recv.at[y], (grp_of(head, zh, core), t)
        )

    def wide_copy(step, head):
        return remote(
            wide_out.at[step], wide_in.at[y], y_send.at[step], y_recv.at[y], (grp_of(head, zh, core), t)
        )

    star = jnp.where(y == head_of(0), 0, jnp.where(y == head_of(1), 1, 2))
    early = jnp.logical_or(star < 2, y == head_of(2))

    def over_z(step, block):
        kept[step] = block
        z_out[step] = block.astype(bf16).reshape(ZH, BLOCK, WIDTH)
        for d in range(1, ZH):
            z_copy(step, d, False).start()

    def z_total(step):
        total = kept[step, pl.ds(pl.multiple_of(zh * BLOCK, BLOCK), BLOCK)]
        for d in range(1, ZH):
            z_copy(step, d, True).wait_recv()
            total = total + z_in[step, lax.rem(zh - d + ZH, ZH)].astype(f32)
        return total

    def from_core(step):
        core_copy(step).wait_recv()
        over_z(step, kept[step] + core_in[step].astype(f32))

    def from_core_wide(step):
        core_copy(step).wait_recv()
        both = kept[step] + core_in[step].astype(f32)
        kept[step] = both
        head = head_of(step)

        @pl.when(head != y)
        def _():
            wide_out[step] = both.astype(bf16)
            wide_copy(step, head).start()

    def from_z(step, _):
        total = z_total(step)
        head = head_of(step)

        @pl.when(head == y)
        def _():
            own_sum[...] = total

        @pl.when(head != y)
        def _():
            y_out[step] = total.astype(bf16)
            y_copy(step, head).start()

        return 0

    def rows_of(step, parity):
        base = head_of(step) * BLOCKS
        return [gathered[base + 2 * k + parity] for k in range(ZH)]

    def multiply(heads):
        lhs = [rows_of(head, 1 - core) + rows_of(head, core) for head in heads]
        result = dot(jnp.concatenate(sum(lhs, []), axis=0), learn[...], ((1,), (0,)))
        for n, head in enumerate(heads):
            core_out[head] = result[2 * n * HALF : (2 * n + 1) * HALF].astype(bf16)
            core_copy(head).start()
            kept[head] = result[(2 * n + 1) * HALF : (2 * n + 2) * HALF]

    def one_step(step, _):
        @pl.when(step == 0)
        def _():
            arrived("r1")

        @pl.when(step == 1)
        def _():
            arrived("z0")
            send("r3")
            arrived("z1")
            send("l3", "r4", "l4")
            arrived("l1")
            send("z4")
            arrived("z2")

        @pl.when(step == 2)
        def _():
            arrived("r2", "l2")
            send("z5")

        @pl.when(step == 3)
        def _():
            arrived("r3", "l3")
            send("r5", "l5")
            arrived("r4", "z3", "l4", "z4")

        @pl.when(step == 4)
        def _():
            arrived("z5", "r5", "l5")

        single = jnp.logical_or(step == 2, step == 4)
        first = 2 * step - jnp.where(step >= 3, 1, 0)

        @pl.when(single)
        def _():
            multiply([first])

        @pl.when(jnp.logical_not(single))
        def _():
            multiply([first, first + 1])

        @pl.when(step == 1)
        def _():
            from_core_wide(0)
            from_core_wide(1)

        @pl.when(step == 2)
        def _():
            from_core_wide(2)
            from_core(3)

        @pl.when(step == 3)
        def _():
            from_core(4)
            from_z(3, 0)
            from_core(5)
            from_core(6)

        @pl.when(step == 4)
        def _():
            from_z(4, 0)

        return 0

    lax.fori_loop(0, 5, one_step, 0)
    from_core(TP - 1)

    def decode_across(at):
        block = decode_all.at[at]
        return remote(block, block, dec_send.at[0], dec_recv.at[0], (grp_of(y, zh, 1 - core), t))

    for d in range(1, Y):
        decode_copy(d, True).wait_recv()
    decode_across(core).start()

    lax.fori_loop(5, TP - 1, from_z, 0)

    @pl.when(early)
    def _():
        block = kept[star]
        for d in range(1, Y):
            source = lax.rem(y - d + Y, Y)
            landed = wide_in.at[source]
            remote(landed, landed, y_send.at[0], y_recv.at[source], (g, right)).wait_recv()
            block = block + wide_in[source].astype(f32)
        over_z(star, block)

    l_queries.wait()
    l_fresh.wait()
    l_keys.wait()
    scale = 1.0 / math.sqrt(HEAD_SIZE)
    tiles = queries[...].astype(f32)
    tiles = jnp.concatenate(
        [tiles[:, j * HEAD_SIZE : (j + 1) * HEAD_SIZE] for j in range(QUERIES)], axis=0
    )
    query_rows = tiles.astype(bf16)
    row_of = lax.broadcasted_iota(jnp.int32, (QUERIES * DECODE, SLOTS), 0) & (DECODE - 1)
    slot_of = lax.broadcasted_iota(jnp.int32, (QUERIES * DECODE, SLOTS), 1)
    scores = jnp.zeros((QUERIES * DECODE, SLOTS), f32)
    for r in range(DECODE):
        of_row = dot(query_rows, keys[r], ((1,), (1,))) * scale
        of_row = jnp.where(slot_of < lengths_ref[r], of_row, -jnp.inf)
        scores = jnp.where(row_of == r, of_row, scores)
    fresh_tiles = jnp.concatenate([fresh[...].astype(f32)] * QUERIES, axis=0)
    own_score = jnp.sum(tiles * fresh_tiles, axis=1, keepdims=True) * scale
    highest = jnp.maximum(jnp.max(scores, axis=1, keepdims=True), own_score)
    cache_exp = jnp.exp(scores - highest)
    own_exp = jnp.exp(own_score - highest)
    denominator = jnp.sum(cache_exp, axis=1, keepdims=True) + own_exp
    weights[...] = (cache_exp / denominator).astype(bf16)
    own_weight = (own_exp / denominator).astype(bf16).astype(f32)
    own_part[...] = jnp.broadcast_to(own_weight, (QUERIES * DECODE, HEAD_SIZE))

    from_z(TP - 1, 0)

    l_values.wait()
    row_at = lax.broadcasted_iota(jnp.int32, (QUERIES * DECODE, HEAD_SIZE), 0) & (DECODE - 1)
    cached = jnp.zeros((QUERIES * DECODE, HEAD_SIZE), f32)
    for r in range(DECODE):
        of_row = dot(weights[...], values[r], ((1,), (0,)))
        cached = jnp.where(row_at == r, of_row, cached)
    cache_part[...] = cached

    for owner in range(ZH):
        fresh_rows[owner * CORE + 1 - core] = jnp.zeros((BLOCK, WIDTH), bf16)

    @pl.when(early)
    def _():
        own_sum[...] = z_total(star)

    @pl.when(jnp.logical_not(early))
    def _():
        total = own_sum[...]
        for d in range(1, Y):
            source = lax.rem(y - d + Y, Y)
            landed = y_in.at[source]
            remote(landed, landed, y_send.at[0], y_recv.at[source], (g, right)).wait_recv()
            total = total + y_in[source].astype(f32)
        own_sum[...] = total

    for load in l_adam:
        load.wait()
    gradient = own_sum[...]

    updated, _, _ = optimizer_step(gradient, adam_in[0], adam_in[1], adam_in[2])

    mine = zh * CORE + core

    def row_copy(d, landed):
        to, source = lax.rem(zh + d, ZH), lax.rem(zh - d + ZH, ZH)
        block = fresh_rows.at[(source if landed else zh) * CORE + core]
        return remote(block, block, row_send.at[d], row_recv.at[d], (grp_of(y, to, core), t))

    fresh_rows[mine] = updated.astype(bf16)
    for d in range(1, ZH):
        row_copy(d, False).start()
    store = pltpu.make_async_copy(own_sum, gradient_hbm, store_sem.at[0])
    store.start()
    decode_across(1 - core).wait_recv()
    decode = decode_all[...].reshape(CORE * Y * DECODE, WIDTH).astype(bf16)
    for d in range(1, ZH):
        row_copy(d, True).wait_recv()

    part = dot(decode, fresh_rows[...].reshape(HEAD_SIZE, WIDTH), ((1,), (1,)))
    part_out[...] = part.reshape(CORE, Y, DECODE, HEAD_SIZE)

    def stays(row, of_core, peer):
        return jnp.logical_and(
            jnp.logical_and(y == t, row == y), jnp.logical_and(of_core == core, peer == t)
        )

    def part_copy(of_core, to):
        return remote(
            part_out.at[of_core, to],
            part_in.at[core, t],
            part_send.at[of_core * Y + to],
            part_recv.at[core * TP + t],
            (grp_of(to, zh, of_core), y),
        )

    for of_core in range(CORE):
        for to in range(Y):

            @pl.when(stays(to, of_core, t))
            def _():
                part_in[core, t] = part_out[of_core, to]

            @pl.when(jnp.logical_not(stays(to, of_core, t)))
            def _():
                part_copy(of_core, to).start()

    for of_core in range(CORE):
        for source in range(TP):

            @pl.when(jnp.logical_not(stays(y, of_core, source)))
            def _():
                landed = part_in.at[of_core, source]
                remote(
                    landed,
                    landed,
                    part_send.at[0],
                    part_recv.at[of_core * TP + source],
                    (grp_of(y, zh, 1 - core), t),
                ).wait_recv()

    new_values = jnp.sum(part_in[...].reshape(CORE * TP, DECODE, HEAD_SIZE), axis=0)
    new_values = new_values.astype(bf16).astype(f32)
    outcome = cache_part[...] + own_part[...] * jnp.concatenate([new_values] * QUERIES, axis=0)
    attended[...] = jnp.concatenate(
        [outcome[j * DECODE : (j + 1) * DECODE] for j in range(QUERIES)], axis=1
    )
    result_store = pltpu.make_async_copy(attended, attended_hbm, store_sem.at[1])
    result_store.start()

    for name in order:
        piece(name, False).wait_send()
    totals_of_core.wait_send()
    for d in range(1, ZH):
        totals_over_z(d, False).wait_send()
        row_copy(d, False).wait_send()
    for d in range(1, Y):
        totals_over_y(d, False).wait_send()
        decode_copy(d, False).wait_send()
    decode_across(core).wait_send()
    for step in range(TP):
        core_copy(step).wait_send()
        head = head_of(step)
        if step >= WIDE:
            for d in range(1, ZH):
                z_copy(step, d, False).wait_send()

        @pl.when(head != y)
        def _():
            (y_copy if step >= WIDE else wide_copy)(step, head).wait_send()

    @pl.when(early)
    def _():
        for d in range(1, ZH):
            z_copy(star, d, False).wait_send()

    for of_core in range(CORE):
        for to in range(Y):

            @pl.when(jnp.logical_not(stays(to, of_core, t)))
            def _():
                part_copy(of_core, to).wait_send()

    store.wait()
    result_store.wait()


def finish_kernel(gradient, master, one, two, attended, new_master, new_one, new_two, rounded):
    new_master[...], new_one[...], new_two[...] = optimizer_step(
        gradient[...], master[...], one[...], two[...]
    )
    rounded[...] = attended[...].astype(bf16)


def per_device(
    learn_rows,
    cot_values,
    rewards,
    group_ids,
    master,
    moment_one,
    moment_two,
    decode_rows,
    queries,
    fresh_keys,
    stored_keys,
    stored_values,
    cache_lengths,
):
    dma = pltpu.SemaphoreType.DMA
    shard = jax.ShapeDtypeStruct((BLOCK, WIDTH), f32)
    heads = QUERIES * HEAD_SIZE
    scratch = [
        ((ROWS, HEAD_SIZE), bf16),
        ((ROWS, WIDTH), bf16),
        ((ROWS // 128, 128), f32),
        ((ROWS // 128, 128), jnp.int32),
        ((3, BLOCK, WIDTH), f32),
        ((DECODE, WIDTH), bf16),
        ((DECODE, heads), bf16),
        ((DECODE, HEAD_SIZE), bf16),
        ((DECODE, SLOTS, HEAD_SIZE), bf16),
        ((DECODE, SLOTS, HEAD_SIZE), bf16),
        ((DECODE, heads), f32),
        ((TP * BLOCKS, BLOCK, ROWS), bf16),
        ((GROUPS, ROWS), bf16),
        ((3, 8, GROUPS), f32),
        ((8, GROUPS), f32),
        ((ZH, 8, GROUPS), f32),
        ((Y, 8, GROUPS), f32),
        ((CORE, Y, DECODE, WIDTH), f32),
        ((QUERIES * DECODE, SLOTS), bf16),
        ((QUERIES * DECODE, HEAD_SIZE), f32),
        ((QUERIES * DECODE, HEAD_SIZE), f32),
        ((TP, HALF, WIDTH), f32),
        ((TP, HALF, WIDTH), bf16),
        ((TP, HALF, WIDTH), bf16),
        ((TP, ZH, BLOCK, WIDTH), bf16),
        ((TP, ZH, BLOCK, WIDTH), bf16),
        ((TP, BLOCK, WIDTH), bf16),
        ((Y, BLOCK, WIDTH), bf16),
        ((WIDE, HALF, WIDTH), bf16),
        ((Y, HALF, WIDTH), bf16),
        ((BLOCK, WIDTH), f32),
        ((ZH * CORE, BLOCK, WIDTH), bf16),
        ((CORE, Y, DECODE, HEAD_SIZE), f32),
        ((CORE, TP, DECODE, HEAD_SIZE), f32),
    ]
    semaphores = [12, 2, 18, 18, TP, TP, TP * ZH, TP * ZH, TP, Y, ZH, ZH, CORE * Y, CORE * TP, ZH + Y, ZH + Y, Y, Y]
    hbm = pl.BlockSpec(memory_space=pltpu.HBM)
    gradient, attended = pl.pallas_call(
        kernel,
        out_shape=(shard, jax.ShapeDtypeStruct((DECODE, heads), f32)),
        in_specs=[hbm] * 12 + [pl.BlockSpec(memory_space=pltpu.SMEM)],
        out_specs=[hbm] * 2,
        scratch_shapes=[pltpu.VMEM(shape, kind) for shape, kind in scratch]
        + [dma((n,)) for n in semaphores],
        compiler_params=pltpu.CompilerParams(
            collective_id=0, has_side_effects=True, vmem_limit_bytes=60 * 1024 * 1024
        ),
    )(
        cot_values,
        learn_rows,
        rewards.reshape(ROWS // 128, 128),
        group_ids.reshape(ROWS // 128, 128),
        master,
        moment_one,
        moment_two,
        decode_rows,
        queries,
        fresh_keys,
        stored_keys,
        stored_values,
        cache_lengths,
    )
    return pl.pallas_call(
        finish_kernel,
        out_shape=(shard, shard, shard, jax.ShapeDtypeStruct((DECODE, heads), bf16)),
    )(gradient, master, moment_one, moment_two, attended)


def solution(mesh):
    shards, rows = P("grp", "tp"), P("grp")
    cache = P("grp", None, "tp")
    in_specs = (
        shards,
        shards,
        rows,
        rows,
        shards,
        shards,
        shards,
        P("grp", None),
        shards,
        shards,
        cache,
        cache,
        rows,
    )
    return jax.shard_map(
        per_device, mesh=mesh, in_specs=in_specs, out_specs=(shards,) * 4, check_vma=False
    )
```

time: 548 us -> 70.3 us (0.13)
  waiting for transfers between devices: 346 us -> 0 us
  blocking collectives: 167 us -> 0 us
  Pallas kernels: 0 us -> 68.3 us
  between operations: 13.8 us -> 0.64 us
  matrix products: 12.9 us -> 0 us
    all_gather x2 -> x0, waiting for transfers between devices: 197 us -> none  [the longest x1 122 us: per_device(): whole_matrix = lax.all_gather(full_width, 'grp', axis=0, tiled=True)]
    reduce_scatter x1 -> x0, waiting for transfers between devices: 149 us -> none  [per_device(): lax.psum_scatter(lax.dot_general(every_column, learn_rows, (((0,), (0,)),...]
    psum x1 -> x0, blocking collectives: 145 us -> none  [per_device(): totals, members = lax.psum((local_totals, local_members), 'grp')]
    pallas_call x0 -> x2, Pallas kernels: none -> 68.3 us  [the longest x1 66.7 us: per_device(): pl.pallas_call(kernel, out_shape=(shard, jax.ShapeDtypeStruct((DECODE, he...]
    all_gather x1 -> x0, blocking collectives: 22.1 us -> none  [per_device(): full_width = lax.all_gather(refreshed, 'tp', axis=1, tiled=True)]
    dot_general x8 -> x0, matrix products: 12.9 us -> none  [the longest x1 6.08 us: per_device(): lax.dot_general(every_column, learn_rows, (((0,), (0,)), ((), ())), prefe...]
  transfers between devices with their start and end apart: 3 -> 0, of which waited for: 3 -> 0; matrix products, arithmetic and copies ran while one was open for 0% -> 0% of each run, Pallas kernels for 0% -> 0%
where the time goes in v1:
time: 70.3 us; the launch traced here: 68.9 us
  Pallas kernels  68.3 us (97%)
    pallas_call x1, Pallas kernels, per_device(): pl.pallas_call(kernel, out_shape=(shard, jax.ShapeDtypeStruct((DECODE, he...  66.7 us
    pallas_call x1, Pallas kernels, per_device(): pl.pallas_call(finish_kernel, out_shape=(shard, shard, shard, jax.ShapeDt...  1.52 us

profile of v1, /device:TPU:7, one launch (start us, length us, event | category | flops | bytes accessed | tf_op | source)
XLA Modules:
  0.0 68.9 jit_solution(5929823693254538608)
XLA Ops:
  0.6 66.7 %shard_map.156 = (f32[16,640]{1,0:T(8,128)}, f32[8,1024]{1,0:T(8,128)}) custom-call(bf16[1536,128]{1,0:T(8,128)(2,1)} %cot_hbm.1, bf16[1536,640]{1,0:T(8,128)(2,1)} %learn_hbm.1, f32[12,128]{1,0:T(8,128)} %bitcast.2, s32[12,128]{1,0:T(8,128)} %bitcast.3, f32[16,640]{1,0:T(8,128)} %master.1, f32[16,640]{1,0:T(8,128)} %one.1, f32[16,640]{1,0:T(8,128)} %two.1, ...), custom_call_target="tpu_custom_call" | custom-call | tf_op jit(solution)/shard_map/pallas_call | solution.py:737
  67.4 1.5 %shard_map.157 = (f32[16,640]{1,0:T(8,128)}, f32[16,640]{1,0:T(8,128)}, f32[16,640]{1,0:T(8,128)}, bf16[8,1024]{1,0:T(8,128)(2,1)}) custom-call(f32[16,640]{1,0:T(8,128)} %get-tuple-element.6.gradient, f32[16,640]{1,0:T(8,128)} %master.1, f32[16,640]{1,0:T(8,128)} %one.1, f32[16,640]{1,0:T(8,128)} %two.1, f32[8,1024]{1,0:T(8,128)} %get-tuple-element.7.attended), custom_call_target="tpu_custom_call" | custom-call | tf_op jit(solution)/shard_map/pallas_call | solution.py:762

commit v2 on v1

--- a/solution.py
+++ b/solution.py
@@ -20,6 +20,8 @@
 BLOCK = 16
 HALF = 64
 WIDE = 3
+FAR_Z = (2, 1, 3)
+FAR_Y = (4, 3, 5, 2, 6, 1, 7)
 
 beta_one = 0.9
 beta_two = 0.95
@@ -161,7 +163,7 @@
         (two_hbm, adam_in.at[2]),
     ]
     loads = [pltpu.make_async_copy(src, dst, load_sem.at[i]) for i, (src, dst) in enumerate(loads)]
-    for load in loads:
+    for load in loads[:3]:
         load.start()
     (l_cot, l_ids, l_rewards, l_queries, l_fresh, l_keys, l_decode, l_learn, l_values, *l_adam) = loads
 
@@ -222,6 +224,8 @@
             piece(name, True).wait_recv()
 
     send("z0", "r0", "l0")
+    for load in loads[3:]:
+        load.start()
 
     l_ids.wait()
     l_rewards.wait()
@@ -256,7 +260,7 @@
             (grp_of(y, to, core), t),
         )
 
-    for d in range(1, ZH):
+    for d in FAR_Z:
         totals_over_z(d, False).start()
     send("z1", "z2")
 
@@ -276,7 +280,7 @@
             (grp_of(to, zh, core), t),
         )
 
-    for d in range(1, Y):
+    for d in FAR_Y:
         totals_over_y(d, False).start()
 
     l_decode.wait()
@@ -368,7 +372,7 @@
     def over_z(step, block):
         kept[step] = block
         z_out[step] = block.astype(bf16).reshape(ZH, BLOCK, WIDTH)
-        for d in range(1, ZH):
+        for d in FAR_Z:
             z_copy(step, d, False).start()
 
     def z_total(step):
@@ -574,72 +578,18 @@
         return remote(block, block, row_send.at[d], row_recv.at[d], (grp_of(y, to, core), t))
 
     fresh_rows[mine] = updated.astype(bf16)
-    for d in range(1, ZH):
+    for d in FAR_Z:
         row_copy(d, False).start()
     store = pltpu.make_async_copy(own_sum, gradient_hbm, store_sem.at[0])
     store.start()
     decode_across(1 - core).wait_recv()
     decode = decode_all[...].reshape(CORE * Y * DECODE, WIDTH).astype(bf16)
-    for d in range(1, ZH):
-        row_copy(d, True).wait_recv()
-
-    part = dot(decode, fresh_rows[...].reshape(HEAD_SIZE, WIDTH), ((1,), (1,)))
-    part_out[...] = part.reshape(CORE, Y, DECODE, HEAD_SIZE)
-
-    def stays(row, of_core, peer):
-        return jnp.logical_and(
-            jnp.logical_and(y == t, row == y), jnp.logical_and(of_core == core, peer == t)
-        )
-
-    def part_copy(of_core, to):
-        return remote(
-            part_out.at[of_core, to],
-            part_in.at[core, t],
-            part_send.at[of_core * Y + to],
-            part_recv.at[core * TP + t],
-            (grp_of(to, zh, of_core), y),
-        )
-
-    for of_core in range(CORE):
-        for to in range(Y):
-
-            @pl.when(stays(to, of_core, t))
-            def _():
-                part_in[core, t] = part_out[of_core, to]
-
-            @pl.when(jnp.logical_not(stays(to, of_core, t)))
-            def _():
-                part_copy(of_core, to).start()
-
-    for of_core in range(CORE):
-        for source in range(TP):
-
-            @pl.when(jnp.logical_not(stays(y, of_core, source)))
-            def _():
-                landed = part_in.at[of_core, source]
-                remote(
-                    landed,
-                    landed,
-                    part_send.at[0],
-                    part_recv.at[of_core * TP + source],
-                    (grp_of(y, zh, 1 - core), t),
-                ).wait_recv()
-
-    new_values = jnp.sum(part_in[...].reshape(CORE * TP, DECODE, HEAD_SIZE), axis=0)
-    new_values = new_values.astype(bf16).astype(f32)
-    outcome = cache_part[...] + own_part[...] * jnp.concatenate([new_values] * QUERIES, axis=0)
-    attended[...] = jnp.concatenate(
-        [outcome[j * DECODE : (j + 1) * DECODE] for j in range(QUERIES)], axis=1
-    )
-    result_store = pltpu.make_async_copy(attended, attended_hbm, store_sem.at[1])
-    result_store.start()
 
     for name in order:
         piece(name, False).wait_send()
     totals_of_core.wait_send()
     for d in range(1, ZH):
         totals_over_z(d, False).wait_send()
-        row_copy(d, False).wait_send()
     for d in range(1, Y):
         totals_over_y(d, False).wait_send()
         decode_copy(d, False).wait_send()
@@ -660,12 +610,74 @@
         for d in range(1, ZH):
             z_copy(star, d, False).wait_send()
 
-    for of_core in range(CORE):
-        for to in range(Y):
-
-            @pl.when(jnp.logical_not(stays(to, of_core, t)))
-            def _():
-                part_copy(of_core, to).wait_send()
+    for d in range(1, ZH):
+        row_copy(d, True).wait_recv()
+
+    part = dot(decode, fresh_rows[...].reshape(HEAD_SIZE, WIDTH), ((1,), (1,)))
+    part_out[...] = part.reshape(CORE, Y, DECODE, HEAD_SIZE)
+
+    def part_copy(of_core, d):
+        to = lax.rem(y + d, Y)
+        return remote(
+            part_out.at[of_core, to],
+            part_in.at[core, t],
+            part_send.at[of_core * Y + to],
+            part_recv.at[core * TP + t],
+            (grp_of(to, zh, of_core), y),
+        )
+
+    for d in FAR_Y:
+        part_copy(core, d).start()
+        part_copy(1 - core, d).start()
+    part_copy(1 - core, 0).start()
+
+    @pl.when(t == y)
+    def _():
+        part_in[core, t] = part_out[core, y]
+
+    @pl.when(t != y)
+    def _():
+        part_copy(core, 0).start()
+
+    def part_arrived(of_core, d):
+        source = lax.rem(t + d, TP)
+        landed = part_in.at[of_core, source]
+        remote(
+            landed,
+            landed,
+            part_send.at[0],
+            part_recv.at[of_core * TP + source],
+            (grp_of(y, zh, 1 - core), t),
+        ).wait_recv()
+
+    for d in range(1, TP):
+        part_arrived(core, d)
+        part_arrived(1 - core, d)
+    part_arrived(1 - core, 0)
+
+    @pl.when(t != y)
+    def _():
+        part_arrived(core, 0)
+
+    new_values = jnp.sum(part_in[...].reshape(CORE * TP, DECODE, HEAD_SIZE), axis=0)
+    new_values = new_values.astype(bf16).astype(f32)
+    outcome = cache_part[...] + own_part[...] * jnp.concatenate([new_values] * QUERIES, axis=0)
+    attended[...] = jnp.concatenate(
+        [outcome[j * DECODE : (j + 1) * DECODE] for j in range(QUERIES)], axis=1
+    )
+    result_store = pltpu.make_async_copy(attended, attended_hbm, store_sem.at[1])
+    result_store.start()
+
+    for d in range(1, ZH):
+        row_copy(d, False).wait_send()
+    for d in range(Y):
+        part_copy(1 - core, d).wait_send()
+    for d in range(1, Y):
+        part_copy(core, d).wait_send()
+
+    @pl.when(t != y)
+    def _():
+        part_copy(core, 0).wait_send()
 
     store.wait()
     result_store.wait()

time: 70.3 us -> 71.2 us (1.013)
  the two profiles are of different devices: /device:TPU:7 before, /device:TPU:5 now
where the time goes in v2:
time: 71.2 us; the launch traced here: 71 us
  Pallas kernels  70.4 us (99%)
    pallas_call x1, Pallas kernels, per_device(): pl.pallas_call(kernel, out_shape=(shard, jax.ShapeDtypeStruct((DECODE, he...  68.9 us
    pallas_call x1, Pallas kernels, per_device(): pl.pallas_call(finish_kernel, out_shape=(shard, shard, shard, jax.ShapeDt...  1.52 us

profile of v2, /device:TPU:5, one launch (start us, length us, event | category | flops | bytes accessed | tf_op | source)
XLA Modules:
  0.0 71.0 jit_solution(18266959468008722338)
XLA Ops:
  0.6 68.9 %shard_map.156 = (f32[16,640]{1,0:T(8,128)}, f32[8,1024]{1,0:T(8,128)}) custom-call(bf16[1536,128]{1,0:T(8,128)(2,1)} %cot_hbm.1, bf16[1536,640]{1,0:T(8,128)(2,1)} %learn_hbm.1, f32[12,128]{1,0:T(8,128)} %bitcast.2, s32[12,128]{1,0:T(8,128)} %bitcast.3, f32[16,640]{1,0:T(8,128)} %master.1, f32[16,640]{1,0:T(8,128)} %one.1, f32[16,640]{1,0:T(8,128)} %two.1, ...), custom_call_target="tpu_custom_call" | custom-call | tf_op jit(solution)/shard_map/pallas_call | solution.py:749
  69.5 1.5 %shard_map.157 = (f32[16,640]{1,0:T(8,128)}, f32[16,640]{1,0:T(8,128)}, f32[16,640]{1,0:T(8,128)}, bf16[8,1024]{1,0:T(8,128)(2,1)}) custom-call(f32[16,640]{1,0:T(8,128)} %get-tuple-element.6.gradient, f32[16,640]{1,0:T(8,128)} %master.1, f32[16,640]{1,0:T(8,128)} %one.1, f32[16,640]{1,0:T(8,128)} %two.1, f32[8,1024]{1,0:T(8,128)} %get-tuple-element.7.attended), custom_call_target="tpu_custom_call" | custom-call | tf_op jit(solution)/shard_map/pallas_call | solution.py:774

commit v3 on v2

--- a/solution.py
+++ b/solution.py
@@ -188,24 +188,23 @@
     xl, xr, xx = tp_of(-1, 0), tp_of(1, 0), tp_of(2, 0)
     zo, zxl, zxr, zxx = tp_of(0, 1), tp_of(-1, 1), tp_of(1, 1), tp_of(2, 1)
     pieces = {
-        "z0": (across, t, zo, 2, 3),
-        "z1": (across, t, zo, 5, 3),
-        "z2": (across, t, zo, 0, 2),
-        "z3": (across, xl, zxl, 0, 2),
-        "z4": (across, xr, zxr, 0, 2),
-        "z5": (across, xx, zxx, 0, 2),
+        "z0": (across, t, zo, 4, 4),
+        "z1": (across, t, zo, 0, 4),
+        "z2": (across, xl, zxl, 0, 1),
+        "z3": (across, xr, zxr, 0, 1),
+        "z4": (across, xx, zxx, 0, 4),
         "r0": (right, t, xl, 0, 4),
         "r1": (right, t, xl, 4, 4),
         "r2": (right, xl, xx, 0, 4),
-        "r3": (right, zo, zxl, 2, 3),
-        "r4": (right, zo, zxl, 5, 3),
-        "r5": (right, zxl, zxx, 2, 3),
+        "r3": (right, zo, zxl, 4, 4),
+        "r4": (right, zo, zxl, 1, 3),
+        "r5": (right, zxl, zxx, 4, 2),
         "l0": (left, t, xr, 4, 4),
         "l1": (left, t, xr, 0, 4),
         "l2": (left, xr, xx, 4, 4),
-        "l3": (left, zo, zxr, 5, 3),
-        "l4": (left, zo, zxr, 2, 3),
-        "l5": (left, zxr, zxx, 5, 3),
+        "l3": (left, zo, zxr, 4, 4),
+        "l4": (left, zo, zxr, 1, 3),
+        "l5": (left, zxr, zxx, 6, 2),
     }
     order = list(pieces)
 
@@ -262,7 +261,7 @@
 
     for d in FAR_Z:
         totals_over_z(d, False).start()
-    send("z1", "z2")
+    send("z1")
 
     total = totals_out[1]
     for d in range(1, ZH):
@@ -295,7 +294,7 @@
         decode_copy(d, False).start()
 
     arrived("r0")
-    send("r2", "z3")
+    send("r2", "z2")
     arrived("l0")
     send("l2")
 
@@ -416,6 +415,42 @@
         base = head_of(step) * BLOCKS
         return [gathered[base + 2 * k + parity] for k in range(ZH)]
 
+    last = TP - 1
+    quarter = HALF // 2
+
+    def last_copy(half):
+        rows = pl.ds(half * quarter, quarter)
+        return remote(
+            core_out.at[last, rows],
+            core_in.at[last, rows],
+            core_send.at[last + half],
+            core_recv.at[last + half],
+            (grp_of(y, zh, 1 - core), t),
+        )
+
+    def multiply_last(half):
+        chosen = slice(half * (ZH // 2), (half + 1) * (ZH // 2))
+        lhs = rows_of(last, 1 - core)[chosen] + rows_of(last, core)[chosen]
+        result = dot(jnp.concatenate(lhs, axis=0), learn[...], ((1,), (0,)))
+        rows = slice(half * quarter, (half + 1) * quarter)
+        core_out[last, rows] = result[:quarter].astype(bf16)
+        last_copy(half).start()
+        kept[last, rows] = result[quarter:]
+
+    def from_core_last(half):
+        last_copy(half).wait_recv()
+        rows = slice(half * quarter, (half + 1) * quarter)
+        both = kept[last, rows] + core_in[last, rows].astype(f32)
+        kept[last, rows] = both
+        blocks = slice(half * (ZH // 2), (half + 1) * (ZH // 2))
+        z_out[last, blocks] = both.astype(bf16).reshape(ZH // 2, BLOCK, WIDTH)
+        for d in FAR_Z:
+            to = lax.rem(zh + d, ZH)
+
+            @pl.when((to >= ZH // 2) if half else (to < ZH // 2))
+            def _():
+                z_copy(last, d, False).start()
+
     def multiply(heads):
         lhs = [rows_of(head, 1 - core) + rows_of(head, core) for head in heads]
         result = dot(jnp.concatenate(sum(lhs, []), axis=0), learn[...], ((1,), (0,)))
@@ -432,36 +467,30 @@
         @pl.when(step == 1)
         def _():
             arrived("z0")
-            send("r3")
+            send("r3", "l3")
+            arrived("l1")
+            send("z3")
             arrived("z1")
-            send("l3", "r4", "l4")
-            arrived("l1")
+            send("r4", "l4")
+
+        @pl.when(step == 2)
+        def _():
+            arrived("r2", "l2")
             send("z4")
-            arrived("z2")
-
-        @pl.when(step == 2)
-        def _():
-            arrived("r2", "l2")
-            send("z5")
 
         @pl.when(step == 3)
         def _():
             arrived("r3", "l3")
             send("r5", "l5")
-            arrived("r4", "z3", "l4", "z4")
-
-        @pl.when(step == 4)
-        def _():
-            arrived("z5", "r5", "l5")
-
-        single = jnp.logical_or(step == 2, step == 4)
+            arrived("r4", "z2", "l4", "z3")
+
         first = 2 * step - jnp.where(step >= 3, 1, 0)
 
-        @pl.when(single)
+        @pl.when(step == 2)
         def _():
             multiply([first])
 
-        @pl.when(jnp.logical_not(single))
+        @pl.when(step != 2)
         def _():
             multiply([first, first + 1])
 
@@ -479,17 +508,18 @@
         def _():
             from_core(4)
             from_z(3, 0)
-            from_core(5)
-            from_core(6)
-
-        @pl.when(step == 4)
-        def _():
-            from_z(4, 0)
 
         return 0
 
-    lax.fori_loop(0, 5, one_step, 0)
-    from_core(TP - 1)
+    lax.fori_loop(0, 4, one_step, 0)
+    arrived("z4")
+    multiply_last(0)
+    from_core(5)
+    from_core(6)
+    from_z(4, 0)
+    from_core_last(0)
+    arrived("r5", "l5")
+    multiply_last(1)
 
     def decode_across(at):
         block = decode_all.at[at]
@@ -498,6 +528,7 @@
     for d in range(1, Y):
         decode_copy(d, True).wait_recv()
     decode_across(core).start()
+    from_core_last(1)
 
     lax.fori_loop(5, TP - 1, from_z, 0)
 
@@ -595,7 +626,11 @@
         decode_copy(d, False).wait_send()
     decode_across(core).wait_send()
     for step in range(TP):
-        core_copy(step).wait_send()
+        if step == last:
+            last_copy(0).wait_send()
+            last_copy(1).wait_send()
+        else:
+            core_copy(step).wait_send()
         head = head_of(step)
         if step >= WIDE:
             for d in range(1, ZH):
@@ -744,7 +779,7 @@
         ((CORE, Y, DECODE, HEAD_SIZE), f32),
         ((CORE, TP, DECODE, HEAD_SIZE), f32),
     ]
-    semaphores = [12, 2, 18, 18, TP, TP, TP * ZH, TP * ZH, TP, Y, ZH, ZH, CORE * Y, CORE * TP, ZH + Y, ZH + Y, Y, Y]
+    semaphores = [12, 2, 17, 17, TP + 1, TP + 1, TP * ZH, TP * ZH, TP, Y, ZH, ZH, CORE * Y, CORE * TP, ZH + Y, ZH + Y, Y, Y]
     hbm = pl.BlockSpec(memory_space=pltpu.HBM)
     gradient, attended = pl.pallas_call(
         kernel,

time: 71.2 us -> 69.8 us (0.980)
  the two profiles are of different devices: /device:TPU:5 before, /device:TPU:7 now
where the time goes in v3:
time: 69.8 us; the launch traced here: 69.2 us
  Pallas kernels  68.5 us (98%)
    pallas_call x1, Pallas kernels, per_device(): pl.pallas_call(kernel, out_shape=(shard, jax.ShapeDtypeStruct((DECODE, he...  67 us
    pallas_call x1, Pallas kernels, per_device(): pl.pallas_call(finish_kernel, out_shape=(shard, shard, shard, jax.ShapeDt...  1.52 us

profile of v3, /device:TPU:7, one launch (start us, length us, event | category | flops | bytes accessed | tf_op | source)
XLA Modules:
  0.0 69.2 jit_solution(15873174248530798022)
XLA Ops:
  0.6 67.0 %shard_map.156 = (f32[16,640]{1,0:T(8,128)}, f32[8,1024]{1,0:T(8,128)}) custom-call(bf16[1536,128]{1,0:T(8,128)(2,1)} %cot_hbm.1, bf16[1536,640]{1,0:T(8,128)(2,1)} %learn_hbm.1, f32[12,128]{1,0:T(8,128)} %bitcast.2, s32[12,128]{1,0:T(8,128)} %bitcast.3, f32[16,640]{1,0:T(8,128)} %master.1, f32[16,640]{1,0:T(8,128)} %one.1, f32[16,640]{1,0:T(8,128)} %two.1, ...), custom_call_target="tpu_custom_call" | custom-call | tf_op jit(solution)/shard_map/pallas_call | solution.py:784
  67.7 1.5 %shard_map.157 = (f32[16,640]{1,0:T(8,128)}, f32[16,640]{1,0:T(8,128)}, f32[16,640]{1,0:T(8,128)}, bf16[8,1024]{1,0:T(8,128)(2,1)}) custom-call(f32[16,640]{1,0:T(8,128)} %get-tuple-element.6.gradient, f32[16,640]{1,0:T(8,128)} %master.1, f32[16,640]{1,0:T(8,128)} %one.1, f32[16,640]{1,0:T(8,128)} %two.1, f32[8,1024]{1,0:T(8,128)} %get-tuple-element.7.attended), custom_call_target="tpu_custom_call" | custom-call | tf_op jit(solution)/shard_map/pallas_call | solution.py:809

commit v4 on v3

--- a/solution.py
+++ b/solution.py
@@ -298,250 +298,6 @@
     arrived("l0")
     send("l2")
 
-    for d in range(1, Y):
-        totals_over_y(d, True).wait_recv()
-        total = total + totals_y[lax.rem(y - d + Y, Y)]
-
-    size = total[3:4]
-    mean = jnp.where(
-        size > 0.5, (total[0:1] + total[1:2] + total[2:3]) / jnp.maximum(size, 1.0), 0.0
-    )
-    high, middle, low = split_three(mean)
-    rows = lax.broadcasted_iota(jnp.int32, (8, GROUPS), 0)
-    stack = jnp.where(
-        rows == 0,
-        high.astype(f32),
-        jnp.where(rows == 1, middle.astype(f32), jnp.where(rows == 2, low.astype(f32), 0.0)),
-    )
-    means = dot(stack.astype(bf16), member[...], ((1,), (0,)))
-    advantage = (reward_row - (means[0:1] + means[1:2] + means[2:3])) / float(ROWS)
-    l_learn.wait()
-    for k in range(ROWS // 128):
-        column = jnp.broadcast_to(advantage[:, k * 128 : (k + 1) * 128], (128, 128)).T
-        scaled = learn[k * 128 : (k + 1) * 128, :].astype(f32) * jnp.concatenate(
-            [column] * (WIDTH // 128), axis=1
-        )
-        learn[k * 128 : (k + 1) * 128, :] = scaled.astype(bf16)
-
-    def head_of(step):
-        x_off = jnp.where(
-            jnp.logical_or(step == 1, step == 5),
-            X - 1,
-            jnp.where(
-                jnp.logical_or(step == 2, step == 6),
-                1,
-                jnp.where(jnp.logical_or(step == 4, step == 7), 2, 0),
-            ),
-        )
-        flip = jnp.where(jnp.logical_or(step == 3, step >= 5), 1, 0)
-        return tp_of(x_off, flip)
-
-    def core_copy(step):
-        return remote(
-            core_out.at[step],
-            core_in.at[step],
-            core_send.at[step],
-            core_recv.at[step],
-            (grp_of(y, zh, 1 - core), t),
-        )
-
-    def z_copy(step, d, landed):
-        to, source = lax.rem(zh + d, ZH), lax.rem(zh - d + ZH, ZH)
-        return remote(
-            z_out.at[step, to],
-            z_in.at[step, source if landed else zh],
-            z_send.at[step * ZH + d],
-            z_recv.at[step * ZH + d],
-            (grp_of(y, to, core), t),
-        )
-
-    def y_copy(step, head):
-        return remote(
-            y_out.at[step], y_in.at[y], y_send.at[step], y_recv.at[y], (grp_of(head, zh, core), t)
-        )
-
-    def wide_copy(step, head):
-        return remote(
-            wide_out.at[step], wide_in.at[y], y_send.at[step], y_recv.at[y], (grp_of(head, zh, core), t)
-        )
-
-    star = jnp.where(y == head_of(0), 0, jnp.where(y == head_of(1), 1, 2))
-    early = jnp.logical_or(star < 2, y == head_of(2))
-
-    def over_z(step, block):
-        kept[step] = block
-        z_out[step] = block.astype(bf16).reshape(ZH, BLOCK, WIDTH)
-        for d in FAR_Z:
-            z_copy(step, d, False).start()
-
-    def z_total(step):
-        total = kept[step, pl.ds(pl.multiple_of(zh * BLOCK, BLOCK), BLOCK)]
-        for d in range(1, ZH):
-            z_copy(step, d, True).wait_recv()
-            total = total + z_in[step, lax.rem(zh - d + ZH, ZH)].astype(f32)
-        return total
-
-    def from_core(step):
-        core_copy(step).wait_recv()
-        over_z(step, kept[step] + core_in[step].astype(f32))
-
-    def from_core_wide(step):
-        core_copy(step).wait_recv()
-        both = kept[step] + core_in[step].astype(f32)
-        kept[step] = both
-        head = head_of(step)
-
-        @pl.when(head != y)
-        def _():
-            wide_out[step] = both.astype(bf16)
-            wide_copy(step, head).start()
-
-    def from_z(step, _):
-        total = z_total(step)
-        head = head_of(step)
-
-        @pl.when(head == y)
-        def _():
-            own_sum[...] = total
-
-        @pl.when(head != y)
-        def _():
-            y_out[step] = total.astype(bf16)
-            y_copy(step, head).start()
-
-        return 0
-
-    def rows_of(step, parity):
-        base = head_of(step) * BLOCKS
-        return [gathered[base + 2 * k + parity] for k in range(ZH)]
-
-    last = TP - 1
-    quarter = HALF // 2
-
-    def last_copy(half):
-        rows = pl.ds(half * quarter, quarter)
-        return remote(
-            core_out.at[last, rows],
-            core_in.at[last, rows],
-            core_send.at[last + half],
-            core_recv.at[last + half],
-            (grp_of(y, zh, 1 - core), t),
-        )
-
-    def multiply_last(half):
-        chosen = slice(half * (ZH // 2), (half + 1) * (ZH // 2))
-        lhs = rows_of(last, 1 - core)[chosen] + rows_of(last, core)[chosen]
-        result = dot(jnp.concatenate(lhs, axis=0), learn[...], ((1,), (0,)))
-        rows = slice(half * quarter, (half + 1) * quarter)
-        core_out[last, rows] = result[:quarter].astype(bf16)
-        last_copy(half).start()
-        kept[last, rows] = result[quarter:]
-
-    def from_core_last(half):
-        last_copy(half).wait_recv()
-        rows = slice(half * quarter, (half + 1) * quarter)
-        both = kept[last, rows] + core_in[last, rows].astype(f32)
-        kept[last, rows] = both
-        blocks = slice(half * (ZH // 2), (half + 1) * (ZH // 2))
-        z_out[last, blocks] = both.astype(bf16).reshape(ZH // 2, BLOCK, WIDTH)
-        for d in FAR_Z:
-            to = lax.rem(zh + d, ZH)
-
-            @pl.when((to >= ZH // 2) if half else (to < ZH // 2))
-            def _():
-                z_copy(last, d, False).start()
-
-    def multiply(heads):
-        lhs = [rows_of(head, 1 - core) + rows_of(head, core) for head in heads]
-        result = dot(jnp.concatenate(sum(lhs, []), axis=0), learn[...], ((1,), (0,)))
-        for n, head in enumerate(heads):
-            core_out[head] = result[2 * n * HALF : (2 * n + 1) * HALF].astype(bf16)
-            core_copy(head).start()
-            kept[head] = result[(2 * n + 1) * HALF : (2 * n + 2) * HALF]
-
-    def one_step(step, _):
-        @pl.when(step == 0)
-        def _():
-            arrived("r1")
-
-        @pl.when(step == 1)
-        def _():
-            arrived("z0")
-            send("r3", "l3")
-            arrived("l1")
-            send("z3")
-            arrived("z1")
-            send("r4", "l4")
-
-        @pl.when(step == 2)
-        def _():
-            arrived("r2", "l2")
-            send("z4")
-
-        @pl.when(step == 3)
-        def _():
-            arrived("r3", "l3")
-            send("r5", "l5")
-            arrived("r4", "z2", "l4", "z3")
-
-        first = 2 * step - jnp.where(step >= 3, 1, 0)
-
-        @pl.when(step == 2)
-        def _():
-            multiply([first])
-
-        @pl.when(step != 2)
-        def _():
-            multiply([first, first + 1])
-
-        @pl.when(step == 1)
-        def _():
-            from_core_wide(0)
-            from_core_wide(1)
-
-        @pl.when(step == 2)
-        def _():
-            from_core_wide(2)
-            from_core(3)
-
-        @pl.when(step == 3)
-        def _():
-            from_core(4)
-            from_z(3, 0)
-
-        return 0
-
-    lax.fori_loop(0, 4, one_step, 0)
-    arrived("z4")
-    multiply_last(0)
-    from_core(5)
-    from_core(6)
-    from_z(4, 0)
-    from_core_last(0)
-    arrived("r5", "l5")
-    multiply_last(1)
-
-    def decode_across(at):
-        block = decode_all.at[at]
-        return remote(block, block, dec_send.at[0], dec_recv.at[0], (grp_of(y, zh, 1 - core), t))
-
-    for d in range(1, Y):
-        decode_copy(d, True).wait_recv()
-    decode_across(core).start()
-    from_core_last(1)
-
-    lax.fori_loop(5, TP - 1, from_z, 0)
-
-    @pl.when(early)
-    def _():
-        block = kept[star]
-        for d in range(1, Y):
-            source = lax.rem(y - d + Y, Y)
-            landed = wide_in.at[source]
-            remote(landed, landed, y_send.at[0], y_recv.at[source], (g, right)).wait_recv()
-            block = block + wide_in[source].astype(f32)
-        over_z(star, block)
-
     l_queries.wait()
     l_fresh.wait()
     l_keys.wait()
@@ -568,8 +324,6 @@
     own_weight = (own_exp / denominator).astype(bf16).astype(f32)
     own_part[...] = jnp.broadcast_to(own_weight, (QUERIES * DECODE, HEAD_SIZE))
 
-    from_z(TP - 1, 0)
-
     l_values.wait()
     row_at = lax.broadcasted_iota(jnp.int32, (QUERIES * DECODE, HEAD_SIZE), 0) & (DECODE - 1)
     cached = jnp.zeros((QUERIES * DECODE, HEAD_SIZE), f32)
@@ -580,6 +334,252 @@
 
     for owner in range(ZH):
         fresh_rows[owner * CORE + 1 - core] = jnp.zeros((BLOCK, WIDTH), bf16)
+
+    for d in range(1, Y):
+        totals_over_y(d, True).wait_recv()
+        total = total + totals_y[lax.rem(y - d + Y, Y)]
+
+    size = total[3:4]
+    mean = jnp.where(
+        size > 0.5, (total[0:1] + total[1:2] + total[2:3]) / jnp.maximum(size, 1.0), 0.0
+    )
+    high, middle, low = split_three(mean)
+    rows = lax.broadcasted_iota(jnp.int32, (8, GROUPS), 0)
+    stack = jnp.where(
+        rows == 0,
+        high.astype(f32),
+        jnp.where(rows == 1, middle.astype(f32), jnp.where(rows == 2, low.astype(f32), 0.0)),
+    )
+    means = dot(stack.astype(bf16), member[...], ((1,), (0,)))
+    advantage = (reward_row - (means[0:1] + means[1:2] + means[2:3])) / float(ROWS)
+    l_learn.wait()
+    for k in range(ROWS // 128):
+        column = jnp.broadcast_to(advantage[:, k * 128 : (k + 1) * 128], (128, 128)).T
+        scaled = learn[k * 128 : (k + 1) * 128, :].astype(f32) * jnp.concatenate(
+            [column] * (WIDTH // 128), axis=1
+        )
+        learn[k * 128 : (k + 1) * 128, :] = scaled.astype(bf16)
+
+    def head_of(step):
+        x_off = jnp.where(
+            jnp.logical_or(step == 1, step == 5),
+            X - 1,
+            jnp.where(
+                jnp.logical_or(step == 2, step == 6),
+                1,
+                jnp.where(jnp.logical_or(step == 4, step == 7), 2, 0),
+            ),
+        )
+        flip = jnp.where(jnp.logical_or(step == 3, step >= 5), 1, 0)
+        return tp_of(x_off, flip)
+
+    def core_copy(step):
+        return remote(
+            core_out.at[step],
+            core_in.at[step],
+            core_send.at[step],
+            core_recv.at[step],
+            (grp_of(y, zh, 1 - core), t),
+        )
+
+    def z_copy(step, d, landed):
+        to, source = lax.rem(zh + d, ZH), lax.rem(zh - d + ZH, ZH)
+        return remote(
+            z_out.at[step, to],
+            z_in.at[step, source if landed else zh],
+            z_send.at[step * ZH + d],
+            z_recv.at[step * ZH + d],
+            (grp_of(y, to, core), t),
+        )
+
+    def y_copy(step, head):
+        return remote(
+            y_out.at[step], y_in.at[y], y_send.at[step], y_recv.at[y], (grp_of(head, zh, core), t)
+        )
+
+    def wide_copy(step, head):
+        return remote(
+            wide_out.at[step], wide_in.at[y], y_send.at[step], y_recv.at[y], (grp_of(head, zh, core), t)
+        )
+
+    star = jnp.where(y == head_of(0), 0, jnp.where(y == head_of(1), 1, 2))
+    early = jnp.logical_or(star < 2, y == head_of(2))
+
+    def over_z(step, block):
+        kept[step] = block
+        z_out[step] = block.astype(bf16).reshape(ZH, BLOCK, WIDTH)
+        for d in FAR_Z:
+            z_copy(step, d, False).start()
+
+    def z_total(step):
+        total = kept[step, pl.ds(pl.multiple_of(zh * BLOCK, BLOCK), BLOCK)]
+        for d in range(1, ZH):
+            z_copy(step, d, True).wait_recv()
+            total = total + z_in[step, lax.rem(zh - d + ZH, ZH)].astype(f32)
+        return total
+
+    def from_core(step):
+        core_copy(step).wait_recv()
+        over_z(step, kept[step] + core_in[step].astype(f32))
+
+    def from_core_wide(step):
+        core_copy(step).wait_recv()
+        both = kept[step] + core_in[step].astype(f32)
+        kept[step] = both
+        head = head_of(step)
+
+        @pl.when(head != y)
+        def _():
+            wide_out[step] = both.astype(bf16)
+            wide_copy(step, head).start()
+
+    def from_z(step, _):
+        total = z_total(step)
+        head = head_of(step)
+
+        @pl.when(head == y)
+        def _():
+            own_sum[...] = total
+
+        @pl.when(head != y)
+        def _():
+            y_out[step] = total.astype(bf16)
+            y_copy(step, head).start()
+
+        return 0
+
+    def rows_of(step, parity):
+        base = head_of(step) * BLOCKS
+        return [gathered[base + 2 * k + parity] for k in range(ZH)]
+
+    last = TP - 1
+    quarter = HALF // 2
+
+    def last_copy(half):
+        rows = pl.ds(half * quarter, quarter)
+        return remote(
+            core_out.at[last, rows],
+            core_in.at[last, rows],
+            core_send.at[last + half],
+            core_recv.at[last + half],
+            (grp_of(y, zh, 1 - core), t),
+        )
+
+    def multiply_last(half):
+        chosen = slice(half * (ZH // 2), (half + 1) * (ZH // 2))
+        lhs = rows_of(last, 1 - core)[chosen] + rows_of(last, core)[chosen]
+        result = dot(jnp.concatenate(lhs, axis=0), learn[...], ((1,), (0,)))
+        rows = slice(half * quarter, (half + 1) * quarter)
+        core_out[last, rows] = result[:quarter].astype(bf16)
+        last_copy(half).start()
+        kept[last, rows] = result[quarter:]
+
+    def from_core_last(half):
+        last_copy(half).wait_recv()
+        rows = slice(half * quarter, (half + 1) * quarter)
+        both = kept[last, rows] + core_in[last, rows].astype(f32)
+        kept[last, rows] = both
+        blocks = slice(half * (ZH // 2), (half + 1) * (ZH // 2))
+        z_out[last, blocks] = both.astype(bf16).reshape(ZH // 2, BLOCK, WIDTH)
+        for d in FAR_Z:
+            to = lax.rem(zh + d, ZH)
+
+            @pl.when((to >= ZH // 2) if half else (to < ZH // 2))
+            def _():
+                z_copy(last, d, False).start()
+
+    def multiply(heads):
+        lhs = [rows_of(head, 1 - core) + rows_of(head, core) for head in heads]
+        result = dot(jnp.concatenate(sum(lhs, []), axis=0), learn[...], ((1,), (0,)))
+        for n, head in enumerate(heads):
+            core_out[head] = result[2 * n * HALF : (2 * n + 1) * HALF].astype(bf16)
+            core_copy(head).start()
+            kept[head] = result[(2 * n + 1) * HALF : (2 * n + 2) * HALF]
+
+    def decode_across(at):
+        block = decode_all.at[at]
+        return remote(block, block, dec_send.at[0], dec_recv.at[0], (grp_of(y, zh, 1 - core), t))
+
+    def one_step(step, _):
+        @pl.when(step == 0)
+        def _():
+            arrived("r1")
+
+        @pl.when(step == 1)
+        def _():
+            arrived("z0")
+            send("r3", "l3")
+            arrived("l1")
+            send("z3")
+            arrived("z1")
+            send("r4", "l4")
+
+        @pl.when(step == 2)
+        def _():
+            arrived("r2", "l2")
+            send("z4")
+
+        @pl.when(step == 3)
+        def _():
+            arrived("r3", "l3")
+            send("r5", "l5")
+            for d in range(1, Y):
+                decode_copy(d, True).wait_recv()
+            decode_across(core).start()
+            arrived("r4", "z2", "l4", "z3")
+
+        first = 2 * step - jnp.where(step >= 3, 1, 0)
+
+        @pl.when(step == 2)
+        def _():
+            multiply([first])
+
+        @pl.when(step != 2)
+        def _():
+            multiply([first, first + 1])
+
+        @pl.when(step == 1)
+        def _():
+            from_core_wide(0)
+            from_core_wide(1)
+
+        @pl.when(step == 2)
+        def _():
+            from_core_wide(2)
+            from_core(3)
+
+        @pl.when(step == 3)
+        def _():
+            from_core(4)
+            from_z(3, 0)
+
+        return 0
+
+    lax.fori_loop(0, 4, one_step, 0)
+    arrived("z4")
+    multiply_last(0)
+    from_core(5)
+    from_core(6)
+    from_z(4, 0)
+    from_core_last(0)
+    arrived("r5", "l5")
+    multiply_last(1)
+
+    from_core_last(1)
+
+    lax.fori_loop(5, TP - 1, from_z, 0)
+
+    @pl.when(early)
+    def _():
+        block = kept[star]
+        for d in range(1, Y):
+            source = lax.rem(y - d + Y, Y)
+            landed = wide_in.at[source]
+            remote(landed, landed, y_send.at[0], y_recv.at[source], (g, right)).wait_recv()
+            block = block + wide_in[source].astype(f32)
+        over_z(star, block)
+
+    from_z(TP - 1, 0)
 
     @pl.when(early)
     def _():

time: 69.8 us -> 70.2 us (level)
  Pallas kernels: 68.5 us -> 69.4 us
    pallas_call x1, Pallas kernels: 67 us -> 67.8 us  [per_device(): pl.pallas_call(kernel, out_shape=(shard, jax.ShapeDtypeStruct((DECODE, he...]
where the time goes in v4:
time: 70.2 us; the launch traced here: 70 us
  Pallas kernels  69.4 us (99%)
    pallas_call x1, Pallas kernels, per_device(): pl.pallas_call(kernel, out_shape=(shard, jax.ShapeDtypeStruct((DECODE, he...  67.8 us
    pallas_call x1, Pallas kernels, per_device(): pl.pallas_call(finish_kernel, out_shape=(shard, shard, shard, jax.ShapeDt...  1.52 us

profile of v4, /device:TPU:7, one launch (start us, length us, event | category | flops | bytes accessed | tf_op | source)
XLA Modules:
  0.0 70.0 jit_solution(13332048489705656276)
XLA Ops:
  0.6 67.8 %shard_map.156 = (f32[16,640]{1,0:T(8,128)}, f32[8,1024]{1,0:T(8,128)}) custom-call(bf16[1536,128]{1,0:T(8,128)(2,1)} %cot_hbm.1, bf16[1536,640]{1,0:T(8,128)(2,1)} %learn_hbm.1, f32[12,128]{1,0:T(8,128)} %bitcast.2, s32[12,128]{1,0:T(8,128)} %bitcast.3, f32[16,640]{1,0:T(8,128)} %master.1, f32[16,640]{1,0:T(8,128)} %one.1, f32[16,640]{1,0:T(8,128)} %two.1, ...), custom_call_target="tpu_custom_call" | custom-call | tf_op jit(solution)/shard_map/pallas_call | solution.py:784
  68.5 1.5 %shard_map.157 = (f32[16,640]{1,0:T(8,128)}, f32[16,640]{1,0:T(8,128)}, f32[16,640]{1,0:T(8,128)}, bf16[8,1024]{1,0:T(8,128)(2,1)}) custom-call(f32[16,640]{1,0:T(8,128)} %get-tuple-element.6.gradient, f32[16,640]{1,0:T(8,128)} %master.1, f32[16,640]{1,0:T(8,128)} %one.1, f32[16,640]{1,0:T(8,128)} %two.1, f32[8,1024]{1,0:T(8,128)} %get-tuple-element.7.attended), custom_call_target="tpu_custom_call" | custom-call | tf_op jit(solution)/shard_map/pallas_call | solution.py:809

commit v5 on v4

--- a/solution.py
+++ b/solution.py
@@ -19,7 +19,7 @@
 BLOCKS = 8
 BLOCK = 16
 HALF = 64
-WIDE = 3
+WIDE = 4
 FAR_Z = (2, 1, 3)
 FAR_Y = (4, 3, 5, 2, 6, 1, 7)
 
@@ -402,8 +402,10 @@
             wide_out.at[step], wide_in.at[y], y_send.at[step], y_recv.at[y], (grp_of(head, zh, core), t)
         )
 
-    star = jnp.where(y == head_of(0), 0, jnp.where(y == head_of(1), 1, 2))
-    early = jnp.logical_or(star < 2, y == head_of(2))
+    star = jnp.where(
+        y == head_of(0), 0, jnp.where(y == head_of(1), 1, jnp.where(y == head_of(2), 2, 3))
+    )
+    early = jnp.logical_or(star < 3, y == head_of(3))
 
     def over_z(step, block):
         kept[step] = block
@@ -546,12 +548,11 @@
         @pl.when(step == 2)
         def _():
             from_core_wide(2)
-            from_core(3)
+            from_core_wide(3)
 
         @pl.when(step == 3)
         def _():
             from_core(4)
-            from_z(3, 0)
 
         return 0
 

time: 70.2 us -> 69.6 us (level)
  Pallas kernels: 69.4 us -> 68.2 us
    pallas_call x1, Pallas kernels: 67.8 us -> 66.7 us  [per_device(): pl.pallas_call(kernel, out_shape=(shard, jax.ShapeDtypeStruct((DECODE, he...]
where the time goes in v5:
time: 69.6 us; the launch traced here: 68.9 us
  Pallas kernels  68.2 us (98%)
    pallas_call x1, Pallas kernels, per_device(): pl.pallas_call(kernel, out_shape=(shard, jax.ShapeDtypeStruct((DECODE, he...  66.7 us
    pallas_call x1, Pallas kernels, per_device(): pl.pallas_call(finish_kernel, out_shape=(shard, shard, shard, jax.ShapeDt...  1.52 us

profile of v5, /device:TPU:7, one launch (start us, length us, event | category | flops | bytes accessed | tf_op | source)
XLA Modules:
  0.0 68.9 jit_solution(18189437107902162755)
XLA Ops:
  0.6 66.7 %shard_map.156 = (f32[16,640]{1,0:T(8,128)}, f32[8,1024]{1,0:T(8,128)}) custom-call(bf16[1536,128]{1,0:T(8,128)(2,1)} %cot_hbm.1, bf16[1536,640]{1,0:T(8,128)(2,1)} %learn_hbm.1, f32[12,128]{1,0:T(8,128)} %bitcast.2, s32[12,128]{1,0:T(8,128)} %bitcast.3, f32[16,640]{1,0:T(8,128)} %master.1, f32[16,640]{1,0:T(8,128)} %one.1, f32[16,640]{1,0:T(8,128)} %two.1, ...), custom_call_target="tpu_custom_call" | custom-call | tf_op jit(solution)/shard_map/pallas_call | solution.py:785
  67.4 1.5 %shard_map.157 = (f32[16,640]{1,0:T(8,128)}, f32[16,640]{1,0:T(8,128)}, f32[16,640]{1,0:T(8,128)}, bf16[8,1024]{1,0:T(8,128)(2,1)}) custom-call(f32[16,640]{1,0:T(8,128)} %get-tuple-element.6.gradient, f32[16,640]{1,0:T(8,128)} %master.1, f32[16,640]{1,0:T(8,128)} %one.1, f32[16,640]{1,0:T(8,128)} %two.1, f32[8,1024]{1,0:T(8,128)} %get-tuple-element.7.attended), custom_call_target="tpu_custom_call" | custom-call | tf_op jit(solution)/shard_map/pallas_call | solution.py:810
